TPU v7x, 32 devices: a whole 2x2x4 slice. The times are simulated.
32 devices in a mesh: band: 16 (over z, x, core), batch: 2 (over y).
Axes of the slice: x: 2, y: 2, z: 4, core: 2. Of those that a mesh axis runs over, the one named last changes fastest.
Arguments:
- incoming_rows: bfloat16 [2, 16384, 512], P('batch', 'band'), may hold values from -6 to 6
- picture_label: int32 [2, 16384], P('batch', 'band'), may hold values from -1 to 12, as said below
- triple_kernel: float32 [512, 1536], P(('band', 'batch')), may hold values from -0.25 to 0.25
- mixer_kernel: float32 [512, 512], P(('band', 'batch')), may hold values from -2 to 2
- widening_kernel: float32 [512, 2048], P(('band', 'batch')), may hold values from -0.25 to 0.25
- narrowing_kernel: float32 [2048, 512], P(('band', 'batch')), may hold values from -0.125 to 0.125
- asker_offset: float32 [512], P(('band', 'batch')), may hold values from -3 to 3
- content_offset: float32 [512], P(('band', 'batch')), may hold values from -3 to 3
- mixer_offset_vector: float32 [512], P(('band', 'batch')), may hold values from -3 to 3
- widening_offset: float32 [2048], P(('band', 'batch')), may hold values from -3 to 3
- narrowing_offset: float32 [512], P(('band', 'batch')), may hold values from -3 to 3
- leading_gain: float32 [512], P(('band', 'batch')), may hold values from 0.5 to 2
- leading_offset: float32 [512], P(('band', 'batch')), may hold values from -2 to 2
- second_gain: float32 [512], P(('band', 'batch')), may hold values from 0.5 to 2
- second_offset: float32 [512], P(('band', 'batch')), may hold values from -2 to 2
- loss_sensitivity: bfloat16 [2, 16384, 512], P('batch', 'band'), may hold values from -6 to 6
Outputs:
- layer_out: bfloat16 [2, 16384, 512], P('batch', 'band')
- input_grad: bfloat16 [2, 16384, 512], P('batch', 'band')
- qkv_grad: float32 [512, 1536], P(('band', 'batch'))
- proj_grad: float32 [512, 512], P(('band', 'batch'))
- expand_grad: float32 [512, 2048], P(('band', 'batch'))
- reduce_grad: float32 [2048, 512], P(('band', 'batch'))
- query_grad: float32 [512], P(('band', 'batch'))
- value_grad: float32 [512], P(('band', 'batch'))
- attn_grad: float32 [512], P(('band', 'batch'))
- hidden_grad: float32 [2048], P(('band', 'batch'))
- mlp_grad: float32 [512], P(('band', 'batch'))
- prescale_grad: float32 [512], P(('band', 'batch'))
- preshift_grad: float32 [512], P(('band', 'batch'))
- midscale_grad: float32 [512], P(('band', 'batch'))
- midshift_grad: float32 [512], P(('band', 'batch'))
Inputs may be any that keep to these rules, and one draw needn't show every extreme that they name: `picture_label`: in every group the first 256 rows of each band of 1024 rows belong to image 0; the rest of a band holds its thumbnails numbered 1, 2, ... in order, 64 rows each, then padding rows marked -1. Thumbnail numbers count within a band only. Every group has a band filled with thumbnails and a band with a single thumbnail.
All inputs are finite; a program needn't handle non-finite values.
Results may differ from a plain program's by a relative error of at most 0.018.
Values may be sent and summed in bfloat16 or wider, within the bound.
No kernel may reach another device: no remote copies, remote signals or barrier semaphores. Data moves between devices by JAX's collectives and lax.ppermute only.
A program may use at most 256 MiB of HBM per device.

v0:
```python
import math

import jax
import jax.numpy as jnp
from jax import lax
from jax.sharding import PartitionSpec as P

HEADS = 8
HEAD = 64
LONG_DEV = 256


epsilon = 1e-06
gelu_scale = 0.7978845608028654


def gelu_tanh(value):
    inner = gelu_scale * (value + 0.044715 * value * value * value)
    return 0.5 * value * (1.0 + jnp.tanh(inner))


def gelu_slope(value):
    inner = gelu_scale * (value + 0.044715 * value * value * value)
    tangent = jnp.tanh(inner)
    return 0.5 * (1.0 + tangent) + 0.5 * value * (1.0 - tangent * tangent) * gelu_scale * (
        1.0 + 3.0 * 0.044715 * value * value
    )


def normalize(matrix, scaling, offset):
    center = matrix - jnp.mean(matrix, axis=1, keepdims=True)
    inverse = lax.rsqrt(jnp.mean(center * center, axis=1, keepdims=True) + epsilon)
    standard = center * inverse
    return (standard * scaling + offset, standard, inverse)


def norm_backward_pass(incoming, standard, inverse, scaling):
    scaled = incoming * scaling
    through = inverse * (
        scaled
        - jnp.mean(scaled, axis=1, keepdims=True)
        - standard * jnp.mean(scaled * standard, axis=1, keepdims=True)
    )
    return (through, jnp.sum(incoming * standard, axis=0), jnp.sum(incoming, axis=0))


def contract_rows(left, right):
    return lax.dot_general(
        left, right, (((0,), (0,)), ((), ())), preferred_element_type=jnp.float32
    )


def contract_cols(left, right):
    return lax.dot_general(
        left, right, (((1,), (1,)), ((), ())), preferred_element_type=jnp.float32
    )


def head_view(matrix):
    return matrix.reshape(matrix.shape[0], HEADS, HEAD)


def score_block(queries, key_block):
    return jnp.einsum("qhd,khd->hqk", queries, key_block, preferred_element_type=jnp.float32) * (
        1.0 / math.sqrt(HEAD)
    )


def grad_block(queries, grad_heads, lse_rows, delta_rows, key_block, value_block, allowed):
    scores = score_block(queries, key_block)
    if allowed is not None:
        scores = jnp.where(allowed[None], scores, -1e30)
    weights = jnp.exp(scores - lse_rows[:, :, None])
    slopes = jnp.einsum("qhd,khd->hqk", grad_heads, value_block, preferred_element_type=jnp.float32)
    score_grad = (weights * (slopes - delta_rows[:, :, None])).astype(jnp.bfloat16)
    return (weights.astype(jnp.bfloat16), score_grad)


def key_side(queries, grad_heads, lse_rows, delta_rows, key_block, value_block):
    weights_low, score_grad = grad_block(
        queries, grad_heads, lse_rows, delta_rows, key_block, value_block, None
    )
    key_grad = jnp.einsum(
        "hqk,qhd->khd", score_grad, queries, preferred_element_type=jnp.float32
    ) * (1.0 / math.sqrt(HEAD))
    value_grad = jnp.einsum(
        "hqk,qhd->khd", weights_low, grad_heads, preferred_element_type=jnp.float32
    )
    return (key_grad, value_grad)


def long_forward(queries, key_heads, value_heads):
    key_total = key_heads.shape[0]
    block_rows = min(key_total, 1024)
    query_count = queries.shape[0]

    def scores_at(turn_index):
        key_block = lax.dynamic_slice_in_dim(key_heads, turn_index * block_rows, block_rows, 0)
        return score_block(queries, key_block)

    def first_pass(turn_index, running):
        running_top, running_sum = running
        scores = scores_at(turn_index)
        new_top = jnp.maximum(running_top, jnp.max(scores, axis=2))
        running_sum = running_sum * jnp.exp(running_top - new_top) + jnp.sum(
            jnp.exp(scores - new_top[:, :, None]), axis=2
        )
        return (new_top, running_sum)

    initial = (
        jnp.full((HEADS, query_count), -1e30, jnp.float32),
        jnp.zeros((HEADS, query_count), jnp.float32),
    )
    running_top, running_sum = lax.fori_loop(0, key_total // block_rows, first_pass, initial)
    lse_rows = running_top + jnp.log(running_sum)

    def second_pass(turn_index, mixed_total):
        weights_low = jnp.exp(scores_at(turn_index) - lse_rows[:, :, None]).astype(jnp.bfloat16)
        value_block = lax.dynamic_slice_in_dim(value_heads, turn_index * block_rows, block_rows, 0)
        return mixed_total + jnp.einsum(
            "hqk,khd->qhd", weights_low, value_block, preferred_element_type=jnp.float32
        )

    mixed_total = lax.fori_loop(
        0, key_total // block_rows, second_pass, jnp.zeros((query_count, HEADS, HEAD), jnp.float32)
    )
    return (mixed_total, lse_rows)


def long_query_pass(queries, key_heads, value_heads, lse_rows, delta_rows, grad_heads):
    key_total = key_heads.shape[0]
    block_rows = min(key_total, 1024)

    def one_turn(turn_index, running):
        key_block = lax.dynamic_slice_in_dim(key_heads, turn_index * block_rows, block_rows, 0)
        value_block = lax.dynamic_slice_in_dim(value_heads, turn_index * block_rows, block_rows, 0)
        unused, score_grad = grad_block(
            queries, grad_heads, lse_rows, delta_rows, key_block, value_block, None
        )
        return running + jnp.einsum(
            "hqk,khd->qhd", score_grad, key_block, preferred_element_type=jnp.float32
        )

    summed = lax.fori_loop(
        0, key_total // block_rows, one_turn, jnp.zeros(queries.shape, jnp.float32)
    )
    return summed * (1.0 / math.sqrt(HEAD))


def short_forward(queries, key_heads, value_heads, segment_ids):
    row_total = queries.shape[0]
    splits = 3 * max(1, row_total // 768)
    block_rows = row_total // splits
    outputs = []
    lse_parts = []
    for split_index in range(splits):
        lower = split_index * block_rows
        allowed = segment_ids[lower : lower + block_rows, None] == segment_ids[None, :]
        scores = jnp.where(
            allowed[None], score_block(queries[lower : lower + block_rows], key_heads), -1e30
        )
        largest = jnp.max(scores, axis=2)
        lse_rows = largest + jnp.log(jnp.sum(jnp.exp(scores - largest[:, :, None]), axis=2))
        weights_low = jnp.exp(scores - lse_rows[:, :, None]).astype(jnp.bfloat16)
        outputs.append(
            jnp.einsum("hqk,khd->qhd", weights_low, value_heads, preferred_element_type=jnp.float32)
        )
        lse_parts.append(lse_rows)
    return (jnp.concatenate(outputs, axis=0), jnp.concatenate(lse_parts, axis=1))


def short_backward(queries, key_heads, value_heads, segment_ids, lse_rows, delta_rows, grad_heads):
    row_total = queries.shape[0]
    splits = 3 * max(1, row_total // 768)
    block_rows = row_total // splits
    query_parts = []
    key_total = jnp.zeros(key_heads.shape, jnp.float32)
    value_total = jnp.zeros(value_heads.shape, jnp.float32)
    for split_index in range(splits):
        lower = split_index * block_rows
        upper = lower + block_rows
        allowed = segment_ids[lower:upper, None] == segment_ids[None, :]
        weights_low, score_grad = grad_block(
            queries[lower:upper],
            grad_heads[lower:upper],
            lse_rows[:, lower:upper],
            delta_rows[:, lower:upper],
            key_heads,
            value_heads,
            allowed,
        )
        query_parts.append(
            jnp.einsum("hqk,khd->qhd", score_grad, key_heads, preferred_element_type=jnp.float32)
            * (1.0 / math.sqrt(HEAD))
        )
        key_total = key_total + jnp.einsum(
            "hqk,qhd->khd", score_grad, queries[lower:upper], preferred_element_type=jnp.float32
        ) * (1.0 / math.sqrt(HEAD))
        value_total = value_total + jnp.einsum(
            "hqk,qhd->khd", weights_low, grad_heads[lower:upper], preferred_element_type=jnp.float32
        )
    return (jnp.concatenate(query_parts, axis=0), key_total, value_total)


def per_device(
    incoming_rows,
    picture_label,
    triple_kernel,
    mixer_kernel,
    widening_kernel,
    narrowing_kernel,
    asker_offset,
    content_offset,
    mixer_offset_vector,
    widening_offset,
    narrowing_offset,
    leading_gain,
    leading_offset,
    second_gain,
    second_offset,
    loss_sensitivity,
):
    copies = (
        lax.all_gather(triple_kernel.astype(jnp.bfloat16), ("band", "batch"), axis=0, tiled=True),
        lax.all_gather(mixer_kernel.astype(jnp.bfloat16), ("band", "batch"), axis=0, tiled=True),
        lax.all_gather(widening_kernel.astype(jnp.bfloat16), ("band", "batch"), axis=0, tiled=True),
        lax.all_gather(
            narrowing_kernel.astype(jnp.bfloat16), ("band", "batch"), axis=0, tiled=True
        ),
        lax.all_gather(asker_offset.astype(jnp.bfloat16), ("band", "batch"), axis=0, tiled=True),
        lax.all_gather(content_offset.astype(jnp.bfloat16), ("band", "batch"), axis=0, tiled=True),
        lax.all_gather(
            mixer_offset_vector.astype(jnp.bfloat16), ("band", "batch"), axis=0, tiled=True
        ),
        lax.all_gather(widening_offset.astype(jnp.bfloat16), ("band", "batch"), axis=0, tiled=True),
        lax.all_gather(
            narrowing_offset.astype(jnp.bfloat16), ("band", "batch"), axis=0, tiled=True
        ),
        lax.all_gather(leading_gain.astype(jnp.bfloat16), ("band", "batch"), axis=0, tiled=True),
        lax.all_gather(leading_offset.astype(jnp.bfloat16), ("band", "batch"), axis=0, tiled=True),
        lax.all_gather(second_gain.astype(jnp.bfloat16), ("band", "batch"), axis=0, tiled=True),
        lax.all_gather(second_offset.astype(jnp.bfloat16), ("band", "batch"), axis=0, tiled=True),
    )
    qkv_full, proj_full, expand_full, reduce_full = (copies[0], copies[1], copies[2], copies[3])
    (
        query_shift,
        value_shift,
        attn_shift,
        hidden_shift,
        mlp_shift,
        gain_one,
        offset_one,
        gain_two,
        offset_two,
    ) = [vector.astype(jnp.float32) for vector in copies[4:]]
    token_rows = incoming_rows[0].astype(jnp.float32)
    segment_ids = picture_label[0]
    live_mask = (segment_ids >= 0).astype(jnp.float32)[:, None]
    upstream = loss_sensitivity[0].astype(jnp.float32)
    width = token_rows.shape[1]
    normed_one, standard_one, inverse_one = normalize(token_rows, gain_one, offset_one)
    normed_low = normed_one.astype(jnp.bfloat16)
    projected = jnp.dot(normed_low, qkv_full, preferred_element_type=jnp.float32)
    queries = (projected[:, :width] + query_shift).astype(jnp.bfloat16)
    keyset = projected[:, width : 2 * width].astype(jnp.bfloat16)
    valueset = (projected[:, 2 * width :] + value_shift).astype(jnp.bfloat16)
    gathered_keys, gathered_values = (
        lax.all_gather(keyset[:LONG_DEV], "band", axis=0, tiled=True),
        lax.all_gather(valueset[:LONG_DEV], "band", axis=0, tiled=True),
    )
    all_key_heads = head_view(gathered_keys)
    all_value_heads = head_view(gathered_values)
    long_queries = head_view(queries[:LONG_DEV])
    long_mixed, long_lse = long_forward(long_queries, all_key_heads, all_value_heads)
    short_queries = head_view(queries[LONG_DEV:])
    short_keys = head_view(keyset[LONG_DEV:])
    short_values = head_view(valueset[LONG_DEV:])
    short_ids = segment_ids[LONG_DEV:]
    short_mixed, short_lse = short_forward(short_queries, short_keys, short_values, short_ids)
    attended = jnp.concatenate([long_mixed, short_mixed], axis=0)
    attended_low = attended.reshape(-1, width).astype(jnp.bfloat16)
    branch_one = jnp.dot(attended_low, proj_full, preferred_element_type=jnp.float32) + attn_shift
    middle = token_rows + live_mask * branch_one
    normed_two, standard_two, inverse_two = normalize(middle, gain_two, offset_two)
    normed_two_low = normed_two.astype(jnp.bfloat16)
    hidden = jnp.dot(normed_two_low, expand_full, preferred_element_type=jnp.float32) + hidden_shift
    active_low = gelu_tanh(hidden).astype(jnp.bfloat16)
    branch_two = jnp.dot(active_low, reduce_full, preferred_element_type=jnp.float32) + mlp_shift
    layer_out = (middle + live_mask * branch_two).astype(jnp.bfloat16)
    branch_grad = (live_mask * upstream).astype(jnp.bfloat16)
    reduce_term = contract_rows(active_low, branch_grad)
    mlp_term = jnp.sum(branch_grad, axis=0, dtype=jnp.float32)
    hidden_grad_low = (contract_cols(branch_grad, reduce_full) * gelu_slope(hidden)).astype(
        jnp.bfloat16
    )
    expand_term = contract_rows(normed_two_low, hidden_grad_low)
    hidden_term = jnp.sum(hidden_grad_low, axis=0, dtype=jnp.float32)
    normed_two_grad = contract_cols(hidden_grad_low, expand_full)
    middle_norm_grad, midscale_term, midshift_term = norm_backward_pass(
        normed_two_grad, standard_two, inverse_two, gain_two
    )
    middle_grad = upstream + middle_norm_grad
    attn_grad_low = (live_mask * middle_grad).astype(jnp.bfloat16)
    proj_term = contract_rows(attended_low, attn_grad_low)
    attn_term = jnp.sum(attn_grad_low, axis=0, dtype=jnp.float32)
    attended_grad = contract_cols(attn_grad_low, proj_full).astype(jnp.bfloat16)
    grad_heads = head_view(attended_grad)
    delta_all = jnp.einsum("qhd,qhd->hq", grad_heads.astype(jnp.float32), attended)
    long_grad = grad_heads[:LONG_DEV]
    long_delta = delta_all[:, :LONG_DEV]
    long_query_grad = long_query_pass(
        long_queries, all_key_heads, all_value_heads, long_lse, long_delta, long_grad
    )
    sub_rows = math.gcd(LONG_DEV * lax.axis_size("band"), 1024)

    def one_block(block_index):
        lower = block_index * sub_rows
        key_block = lax.dynamic_slice_in_dim(all_key_heads, lower, sub_rows, 0)
        value_block = lax.dynamic_slice_in_dim(all_value_heads, lower, sub_rows, 0)
        key_grad, value_grad = key_side(
            long_queries, long_grad, long_lse, long_delta, key_block, value_block
        )
        return jnp.concatenate(
            [key_grad.reshape(sub_rows, width), value_grad.reshape(sub_rows, width)], axis=1
        )

    stacked = lax.map(
        one_block, jnp.arange(LONG_DEV * lax.axis_size("band") // sub_rows, dtype=jnp.int32)
    )
    summed = lax.psum_scatter(
        stacked.reshape(LONG_DEV * lax.axis_size("band"), 2 * width).astype(jnp.bfloat16),
        "band",
        scatter_dimension=0,
        tiled=True,
    ).astype(jnp.float32)
    long_key_grad = summed[:, :width]
    long_value_grad = summed[:, width:]
    short_query_grad, short_key_grad, short_value_grad = short_backward(
        short_queries,
        short_keys,
        short_values,
        short_ids,
        short_lse,
        delta_all[:, LONG_DEV:],
        grad_heads[LONG_DEV:],
    )
    query_grad_low = jnp.concatenate(
        [long_query_grad.reshape(-1, width), short_query_grad.reshape(-1, width)], axis=0
    ).astype(jnp.bfloat16)
    key_grad_low = jnp.concatenate(
        [long_key_grad, short_key_grad.reshape(-1, width)], axis=0
    ).astype(jnp.bfloat16)
    value_grad_low = jnp.concatenate(
        [long_value_grad, short_value_grad.reshape(-1, width)], axis=0
    ).astype(jnp.bfloat16)
    qkv_grad_low = jnp.concatenate([query_grad_low, key_grad_low, value_grad_low], axis=1)
    qkv_term = contract_rows(normed_low, qkv_grad_low)
    query_term = jnp.sum(query_grad_low, axis=0, dtype=jnp.float32)
    value_term = jnp.sum(value_grad_low, axis=0, dtype=jnp.float32)
    normed_one_grad = contract_cols(qkv_grad_low, qkv_full)
    input_normed_gradient, prenorm_scale_term, prenorm_shift_term = norm_backward_pass(
        normed_one_grad, standard_one, inverse_one, gain_one
    )
    input_grad = (middle_grad + input_normed_gradient).astype(jnp.bfloat16)
    ordered = (
        lax.psum_scatter(qkv_term, ("band", "batch"), scatter_dimension=0, tiled=True),
        lax.psum_scatter(proj_term, ("band", "batch"), scatter_dimension=0, tiled=True),
        lax.psum_scatter(expand_term, ("band", "batch"), scatter_dimension=0, tiled=True),
        lax.psum_scatter(reduce_term, ("band", "batch"), scatter_dimension=0, tiled=True),
        lax.psum_scatter(query_term, ("band", "batch"), scatter_dimension=0, tiled=True),
        lax.psum_scatter(value_term, ("band", "batch"), scatter_dimension=0, tiled=True),
        lax.psum_scatter(attn_term, ("band", "batch"), scatter_dimension=0, tiled=True),
        lax.psum_scatter(hidden_term, ("band", "batch"), scatter_dimension=0, tiled=True),
        lax.psum_scatter(mlp_term, ("band", "batch"), scatter_dimension=0, tiled=True),
        lax.psum_scatter(prenorm_scale_term, ("band", "batch"), scatter_dimension=0, tiled=True),
        lax.psum_scatter(prenorm_shift_term, ("band", "batch"), scatter_dimension=0, tiled=True),
        lax.psum_scatter(midscale_term, ("band", "batch"), scatter_dimension=0, tiled=True),
        lax.psum_scatter(midshift_term, ("band", "batch"), scatter_dimension=0, tiled=True),
    )
    return (
        layer_out[None],
        input_grad[None],
        ordered[0],
        ordered[1],
        ordered[2],
        ordered[3],
        ordered[4],
        ordered[5],
        ordered[6],
        ordered[7],
        ordered[8],
        ordered[9],
        ordered[10],
        ordered[11],
        ordered[12],
    )


def solution(mesh):
    in_specs = (
        P("batch", "band", None),
        P("batch", "band"),
        P(("band", "batch"), None),
        P(("band", "batch"), None),
        P(("band", "batch"), None),
        P(("band", "batch"), None),
        P(("band", "batch")),
        P(("band", "batch")),
        P(("band", "batch")),
        P(("band", "batch")),
        P(("band", "batch")),
        P(("band", "batch")),
        P(("band", "batch")),
        P(("band", "batch")),
        P(("band", "batch")),
        P("batch", "band", None),
    )
    out_specs = (
        P("batch", "band", None),
        P("batch", "band", None),
        P(("band", "batch"), None),
        P(("band", "batch"), None),
        P(("band", "batch"), None),
        P(("band", "batch"), None),
        P(("band", "batch")),
        P(("band", "batch")),
        P(("band", "batch")),
        P(("band", "batch")),
        P(("band", "batch")),
        P(("band", "batch")),
        P(("band", "batch")),
        P(("band", "batch")),
        P(("band", "batch")),
    )
    return jax.shard_map(
        per_device, mesh=mesh, in_specs=in_specs, out_specs=out_specs, check_vma=False
    )
```

profile of v0, /device:TPU:0, one launch (start us, length us, event | category | flops | bytes accessed | tf_op | source)
XLA Modules:
  0.0 1058.3 jit_solution(9352334031853828921)
XLA Ops:
  16.7 42.2 %all-reduce.19 = (bf16[512]{0:T(512)(128)(2,1)S(1)}, bf16[512]{0:T(512)(128)(2,1)S(1)}, bf16[512]{0:T(512)(128)(2,1)S(1)}, bf16[512]{0:T(512)(128)(2,1)S(1)}, bf...) all-reduce(bf16[512]{0:T(512)(128)(2,1)S(1)} %dynamic-update-slice., ...), channel_id=1, replica_groups=mesh['band'=16,'batch'=2] {'band','batch'}, use_global_device_ids=true, to_apply=%add.1 | all-reduce | flops 6144 | bytes 24576
  60.9 8.4 all-gather.6.cloned.1.call-done
  69.4 6.1 fusion.117
  77.9 3.8 fusion.82
  84.1 76.1 %all_gather.52 = bf16[512,512]{1,0:T(8,128)(2,1)} all-gather(bf16[16,512]{1,0:T(8,128)(2,1)S(1)} %convert_element_type.214), channel_id=1, replica_groups=mesh['band'=16,'batch'=2] {'band','batch'}, dimensions={0}, use_global_device_ids=true | all-gather | bytes 540672 | tf_op jit(solution)/shard_map/all_gather | solution.py:225
  181.3 3.0 exponential_reduce_fusion
  187.0 2.6 convolution_bitcast_fusion.1
  192.2 6.4 copy.93
  198.6 16.3 %while.55 = (s32[]{:T(128)}, f32[8,256]{1,0:T(8,128)S(1)}, f32[8,256]{1,0:T(8,128)S(1)}, bf16[4096,8,64]{0,2,1:T(8,128)(2,1)}, bf16[256,8,64]{0,2,1:T(8,128)(2,1...) while((s32[]{:T(128)}, f32[8,256]{1,0:T(8,128)S(1)}, f32[8,256]{1,0:T(8,128)S(1)}, ...), condition=%wide.region_5.0_spmd.clone, body=%wide.region_2.0_spmd.clone.sunk | while | flops 278931456 | bytes 18194592 | solution.py:114
  214.9 6.5 copy.92
  221.4 16.3 %while.56 = (s32[]{:T(128)}, f32[256,8,64]{0,2,1:T(8,128)S(1)}, bf16[4096,8,64]{0,2,1:T(8,128)(2,1)}, bf16[4096,8,64]{0,2,1:T(8,128)(2,1)}, bf16[256,8,64]{0,2,1...) while((s32[]{:T(128)}, f32[256,8,64]{0,2,1:T(8,128)S(1)}, ...), condition=%wide.region_7.0_spmd.clone, body=%wide.region_6.0_spmd.clone.sunk | while | flops 543424512 | bytes 3417764 | solution.py:124
  221.5 4.0 fusion.216
  225.5 4.0 fusion.216
  229.6 4.0 fusion.216
  233.7 4.0 fusion.216
  244.3 8.1 fusion.111
  252.4 45.5 %all-gather.14.cloned.1.call-done = bf16[2048,512]{1,0:T(8,128)(2,1)} async-done(((bf16[64,512]{1,0:T(8,128)(2,1)}), bf16[2048,512]{1,0:T(8,128)(2,1)}) %all-gather.14.cloned.1.call-update) | async-done | bytes 2097168 | tf_op jit(solution)/shard_map/all_gather | solution.py:227
  297.9 11.3 %convert_reduce_fusion = (f32[2048]{0:T(1024)}, bf16[1024,2048]{1,0:T(8,128)(2,1)S(1)}) fusion(f32[1024,2048]{1,0:T(8,128)} %fusion.111, f32[2048]{0:T(1024)S(1)} %convert_element_type.224, bf16[2048,512]{1,0:T(8,128)(2,1)} %all-gather.14.cloned.1.call-done, bf16[1,1024,512]{1,2,0:T(8,128)(2,1)S(1)} %copy.101, f32[1024]{0:T(1024)S(1)} %bitcast.266), kind=kOutput, calls=%fused_computation.60 | convolution fusion | flops 2195191808 | bytes 15749120 | tf_op jit(solution)/shard_map/dot_general | solution.py:54
  309.2 4.3 fusion.120
  313.5 3.0 copy.102
  316.5 3.0 multiply_reduce_fusion
  323.2 99.5 %while.54 = (s32[]{:T(128)}, bf16[4,1024,1024]{2,1,0:T(8,128)(2,1)}, s32[4]{0:T(128)S(1)}, bf16[4096,8,64]{0,2,1:T(8,128)(2,1)}, bf16[256,8,64]{0,2,1:T(8,128)(2...) while((s32[]{:T(128)}, ...), condition=%wide.region_21.22_spmd, body=%wide.region_20.21_spmd.sunk | while | flops 1095761920 | bytes 43016396 | solution.py:327
  324.6 5.8 fusion.207
  330.4 6.9 fusion.209
  337.3 4.9 fusion.208
  343.8 2.9 copy.142
  349.4 5.8 fusion.207
  355.3 6.9 fusion.209
  362.2 4.9 fusion.208
  368.7 2.9 copy.142
  374.4 5.8 fusion.207
  380.2 6.9 fusion.209
  387.1 4.9 fusion.208
  393.6 2.9 copy.142
  399.2 5.8 fusion.207
  405.0 6.9 fusion.209
  411.9 4.9 fusion.208
  418.4 2.9 copy.142
  424.0 3.0 fusion.123
  427.1 10.7 %fusion.94 = f32[2048,512]{1,0:T(8,128)} fusion(bf16[1,1024,512]{1,2,0:T(8,128)(2,1)S(1)} %copy-done.18, f32[1024]{0:T(1024)S(1)} %bitcast.268, f32[1024,2048]{1,0:T(8,128)} %fusion.111, f32[2048]{0:T(1024)S(1)} %convert_element_type.224), kind=kOutput, calls=%fused_computation.141 | convolution fusion | flops 2170028032 | bytes 13643776 | tf_op jit(solution)/shard_map/dot_general | solution.py:48
  439.2 5.0 multiply_convert_fusion.12
  446.0 4.3 multiply_convert_fusion.11
  457.2 4.5 fusion.110
  462.7 51.9 %while.57 = (s32[]{:T(128)}, f32[256,8,64]{0,2,1:T(8,128)S(1)}, bf16[4096,8,64]{0,2,1:T(8,128)(2,1)}, bf16[256,8,64]{0,2,1:T(8,128)(2,1)S(1)}, f32[8,256]{1,0:T(...) while((s32[]{:T(128)}, f32[256,8,64]{0,2,1:T(8,128)S(1)}, ...), condition=%wide.region_19.20_spmd.clone, body=%wide.region_18.19_spmd.clone.sunk | while | flops 816054272 | bytes 21513912 | solution.py:144
  463.1 5.8 fusion.222
  468.9 7.1 fusion.223
  476.0 5.8 fusion.222
  481.8 7.1 fusion.223
  488.9 5.9 fusion.222
  494.8 7.0 fusion.223
  501.8 5.8 fusion.222
  507.6 6.9 fusion.223
  516.6 3.3 fusion.122
  526.8 2.9 add_convert_fusion.2
  532.5 5.5 fusion.105
  538.0 8.7 fusion.85
  550.3 5.5 fusion.119
  555.8 3.0 copy.106
  562.5 39.1 %all-reduce.18 = (f32[512]{0:T(512)S(1)}, f32[512]{0:T(512)S(1)}, f32[512]{0:T(512)S(1)}, f32[2048]{0:T(1024)S(1)}, f32[512]{0:T(512)S(1)}, /*index=5*/f32[512]{...) all-reduce(f32[512]{0:T(512)S(1)} %convert_reduce_fusion.5, ...), channel_id=7, replica_groups=mesh['band'=16,'batch'=2] {'band','batch'}, use_global_device_ids=true, to_apply=%region_30.31.clone | all-reduce | flops 6144 | bytes 49152
  606.3 4.9 fusion.93
  614.1 50.0 %reduce-scatter.10.cloned.1.call-done = f32[16,512]{1,0:T(8,128)} async-done(((f32[512,512]{1,0:T(8,128)}), f32[16,512]{1,0:T(8,128)}) %reduce-scatter.10.cloned.1.call-update) | async-done | bytes 32784 | tf_op jit(solution)/shard_map/reduce_scatter | solution.py:367
  664.2 140.4 %reduce-scatter.14.cloned.1.call-done = f32[64,512]{1,0:T(8,128)} async-done(((f32[2048,512]{1,0:T(8,128)}), f32[64,512]{1,0:T(8,128)}) %reduce-scatter.14.cloned.1.call-update) | async-done | bytes 131088 | tf_op jit(solution)/shard_map/reduce_scatter | solution.py:369
  804.6 141.4 %reduce-scatter.12.cloned.1.call-done = f32[16,2048]{1,0:T(8,128)} async-done(((f32[512,2048]{1,0:T(8,128)}), f32[16,2048]{1,0:T(8,128)}) %reduce-scatter.12.cloned.1.call-update) | async-done | bytes 131088 | tf_op jit(solution)/shard_map/reduce_scatter | solution.py:368
  945.9 105.3 %reduce-scatter.8.cloned.1.call-done = f32[16,1536]{1,0:T(8,128)} async-done(((f32[512,1536]{1,0:T(8,128)}), f32[16,1536]{1,0:T(8,128)}) %reduce-scatter.8.cloned.1.call-update) | async-done | bytes 98320 | tf_op jit(solution)/shard_map/reduce_scatter | solution.py:366
  (359 shorter events, 121.4 us)
Async XLA Ops:
  7.2 62.2 %all-gather.6.cloned.1.call-start = ((), (), s32[]{:S(2)}) async-start(), calls=%async_computation.5 | async-start | bytes 1622016 | tf_op jit(solution)/shard_map/all_gather | solution.py:224
  8.8 183.4 %all-gather.10.cloned.1.call-start = ((), (), s32[]{:S(2)}) async-start(), calls=%async_computation.7 | async-start | bytes 4456448 | tf_op jit(solution)/shard_map/all_gather | solution.py:268
  58.9 16.6 %copy-start.68 = (f32[512]{0:T(512)}, f32[512]{0:T(512)S(1)}, u32[]{:S(2)}) copy-start(f32[512]{0:T(512)S(1)} %convert_element_type.200) | copy-start | bytes 6148
  58.9 16.6 %copy-start.58 = (f32[512]{0:T(512)}, f32[512]{0:T(512)S(1)}, u32[]{:S(2)}) copy-start(f32[512]{0:T(512)S(1)} %convert_element_type.198) | copy-start | bytes 6148
  60.4 179.9 %copy-start.1 = (bf16[1,1024,512]{1,2,0:T(8,128)(2,1)}, bf16[1,1024,512]{1,2,0:T(8,128)(2,1)S(1)}, u32[]{:S(2)}) copy-start(bf16[1,1024,512]{1,2,0:T(8,128)(2,1)S(1)} %copy.91) | copy-start | bytes 3145732
  60.6 14.9 %copy-start.48 = (f32[1024]{0:T(1024)}, f32[1024]{0:T(1024)S(1)}, u32[]{:S(2)}) copy-start(f32[1024]{0:T(1024)S(1)} %broadcast_multiply_fusion.5) | copy-start | bytes 12292
  60.9 14.5 %copy-start.54 = (f32[1024]{0:T(1024)}, f32[1024]{0:T(1024)S(1)}, u32[]{:S(2)}) copy-start(f32[1024]{0:T(1024)S(1)} %add_rsqrt_fusion.1) | copy-start | bytes 12292
  75.5 7.0 copy-start.56
  75.5 7.7 copy-start.57
  77.1 6.8 copy-start.67
  77.1 7.0 copy-start.66
  77.9 137.1 %all-gather.8.cloned.1.call-start = ((), (), s32[]{:S(2)}) async-start(), calls=%async_computation.6 | async-start | bytes 4456448 | tf_op jit(solution)/shard_map/all_gather | solution.py:269
  82.5 161.8 %all-gather.12.cloned.1.call-start = ((), (), s32[]{:S(2)}) async-start(), calls=%async_computation.8 | async-start | bytes 2162688 | tf_op jit(solution)/shard_map/all_gather | solution.py:226
  83.2 214.7 %all-gather.14.cloned.1.call-start = ((), (), s32[]{:S(2)}) async-start(), calls=%async_computation.9 | async-start | bytes 2162688 | tf_op jit(solution)/shard_map/all_gather | solution.py:227
  83.9 445.8 %reduce-scatter.6.cloned.1.call-start = ((), (), s32[]{:S(2)}) async-start(), calls=%async_computation.10 | async-start | bytes 8912896 | tf_op jit(solution)/shard_map/reduce_scatter | solution.py:330
  161.7 157.9 %copy-start.17 = (bf16[1,1024,512]{1,2,0:T(8,128)(2,1)}, bf16[1,1024,512]{1,2,0:T(8,128)(2,1)S(1)}, u32[]{:S(2)}) copy-start(bf16[1,1024,512]{1,2,0:T(8,128)(2,1)S(1)} %copy.101) | copy-start | bytes 3145732
  161.7 4.3 copy-start.20
  163.8 7.9 copy-start.21
  171.7 5.1 copy-start.28
  174.3 5.5 copy-start.3
  176.8 7.5 copy-start.10
  178.5 5.8 copy-start.73
  179.8 7.1 copy-start.11
  181.2 8.3 copy-start
  184.3 5.3 copy-start.64
  214.9 6.5 copy-start.45
  240.3 12.1 %copy-start.34 = (bf16[1024,8,64]{0,2,1:T(8,128)(2,1)}, bf16[1024,8,64]{0,2,1:T(8,128)(2,1)S(1)}, u32[]{:S(2)}) copy-start(bf16[1024,8,64]{0,2,1:T(8,128)(2,1)S(1)} %fusion.86) | copy-start | bytes 3145732
  297.9 11.3 %copy-start.80 = (bf16[512,2048]{1,0:T(8,128)(2,1)S(1)}, bf16[512,2048]{1,0:T(8,128)(2,1)}, u32[]{:S(2)}) copy-start(bf16[512,2048]{1,0:T(8,128)(2,1)} %all-gather.12.cloned.1.call-done) | copy-start | bytes 6291460
  309.2 4.3 copy-start.81
  422.8 4.3 copy-start.18
  422.8 241.4 %reduce-scatter.10.cloned.1.call-start = ((), (), s32[]{:S(2)}) async-start(), calls=%async_computation.12 | async-start | bytes 1081344 | tf_op jit(solution)/shard_map/reduce_scatter | solution.py:367
  427.0 377.5 %reduce-scatter.14.cloned.1.call-start = ((), (), s32[]{:S(2)}) async-start(), calls=%async_computation.14 | async-start | bytes 4325376 | tf_op jit(solution)/shard_map/reduce_scatter | solution.py:369
  437.8 508.1 %reduce-scatter.12.cloned.1.call-start = ((), (), s32[]{:S(2)}) async-start(), calls=%async_computation.13 | async-start | bytes 4325376 | tf_op jit(solution)/shard_map/reduce_scatter | solution.py:368
  439.2 5.0 copy-start.4
  439.2 12.3 %slice-start.2 = ((s8[6291456]{0:T(1024)(128)(4,1)}), s8[4194304]{0:T(1024)(128)(4,1)S(1)}, s32[]{:S(2)}) async-start(s8[6291456]{0:T(1024)(128)(4,1)} %bitcast.225), calls=%async_computation.17 | async-start | bytes 8388608
  446.0 5.5 slice-start.3
  450.4 3.9 copy-start.12
  451.8 4.1 copy-start.82
  461.7 589.6 %reduce-scatter.8.cloned.1.call-start = ((), (), s32[]{:S(2)}) async-start(), calls=%async_computation.11 | async-start | bytes 3244032 | tf_op jit(solution)/shard_map/reduce_scatter | solution.py:366
  462.7 53.9 %copy-start.27 = (bf16[256,512]{0,1:T(8,128)(2,1)S(1)}, bf16[256,512]{0,1:T(8,128)(2,1)}, u32[]{:S(2)}) copy-start(bf16[256,512]{0,1:T(8,128)(2,1)} %copy.98) | copy-start | bytes 786436
  515.4 4.5 copy-start.16
  515.4 4.6 copy-start.29
  515.4 5.2 copy-start.13
  515.4 5.3 copy-start.25
  516.6 5.6 slice-start.6
  516.6 8.3 slice-start.4
  519.9 3.4 slice-start.7
  519.9 3.3 copy-start.53
  520.6 4.3 slice-start.5
  523.3 3.4 slice-start
  526.8 5.7 copy-start.2
  526.8 5.7 copy-start.49
  526.8 5.7 copy-start.55
  526.8 5.7 copy-start.59
  526.8 5.7 copy-start.69
  532.5 5.5 copy-start.79
  532.5 5.5 copy-start.8
  555.8 6.7 copy-start.70
  555.8 6.7 copy-start.71
  555.8 6.7 copy-start.72
  555.8 6.7 copy-start.77
  555.8 6.7 copy-start.78
  555.8 50.5 %copy-start.61 = (f32[1024]{0:T(1024)S(1)}, f32[1024]{0:T(1024)}, u32[]{:S(2)}) copy-start(f32[1024]{0:T(1024)} %copy-done.60) | copy-start | bytes 12292
  555.8 50.5 %copy-start.63 = (f32[1024]{0:T(1024)S(1)}, f32[1024]{0:T(1024)}, u32[]{:S(2)}) copy-start(f32[1024]{0:T(1024)} %copy-done.62) | copy-start | bytes 12292
  (37 other events, 69.4 us)
Sparse Core Ops, SparseCore 0:
  11.5 57.8 all-gather.5
  78.0 50.7 all-gather.9
  130.9 49.3 all-gather.7
  183.9 55.0 all-gather.11
  242.5 55.3 all-gather.13
  422.9 103.4 reduce-scatter.5
  529.2 134.9 reduce-scatter.9
  667.1 137.4 reduce-scatter.13
  807.5 138.3 reduce-scatter.11
  952.7 98.5 reduce-scatter.7
where the time goes:
time: 1070 us; the launch traced here: 1060 us
  waiting for transfers between devices  491 us (46%)
  matrix products  259 us (24%)
  blocking collectives  157 us (15%)
  local copies, waits for them, and re-layouts  81.4 us (8%)
  other arithmetic  49.8 us (5%)
  between operations  15.6 us (1%)
    reduce_scatter x1, waiting for transfers between devices, per_device(): lax.psum_scatter(expand_term, ('band', 'batch'), scatter_dimension=0, til...  141 us
    reduce_scatter x1, waiting for transfers between devices, per_device(): lax.psum_scatter(reduce_term, ('band', 'batch'), scatter_dimension=0, til...  140 us
    reduce_scatter x1, waiting for transfers between devices, per_device(): lax.psum_scatter(qkv_term, ('band', 'batch'), scatter_dimension=0, tiled=...  105 us
    unnamed x2, blocking collectives  81.3 us
    all_gather x1, blocking collectives, per_device(): lax.all_gather(mixer_kernel.astype(jnp.bfloat16), ('band', 'batch'), axis...  76.1 us
    dot_general x15, matrix products, score_block(): jnp.einsum('qhd,khd->hqk', queries, key_block, preferred_element_type=jnp...  61.9 us
    reduce_scatter x1, waiting for transfers between devices, per_device(): lax.psum_scatter(proj_term, ('band', 'batch'), scatter_dimension=0, tiled...  50 us
    all_gather x1, waiting for transfers between devices, per_device(): lax.all_gather(narrowing_kernel.astype(jnp.bfloat16), ('band', 'batch'),...  45.5 us
  transfers between devices with their start and end apart: 10, of which 6 were waited for; matrix products, arithmetic and copies ran while one was open for 23% of the time, Pallas kernels for 0%

commit v1 on v0

v1 whole, which is shorter than its diff:
```python
import functools
import math

import jax
import jax.numpy as jnp
from jax import lax
from jax.experimental import pallas as pl
from jax.experimental.pallas import tpu as pltpu
from jax.sharding import PartitionSpec as P

HEADS = 8
HEAD = 64
LONG = 256
WIDTH = 512
FF = 2048
GROUP = 256
TILE = 512
epsilon = 1e-06
gelu_scale = 0.7978845608028654
f32 = jnp.float32
bf16 = jnp.bfloat16
PARAMS = dict(vmem_limit_bytes=58 << 20)


def dot(left, right, cl=1, cr=0):
    return lax.dot_general(left, right, (((cl,), (cr,)), ((), ())), preferred_element_type=f32)


def standardize(rows):
    center = rows - jnp.mean(rows, axis=1, keepdims=True)
    inverse = lax.rsqrt(jnp.mean(center * center, axis=1, keepdims=True) + epsilon)
    return center * inverse, inverse


def norm_backward(incoming, standard, inverse, scaling):
    scaled = incoming * scaling
    return inverse * (
        scaled
        - jnp.mean(scaled, axis=1, keepdims=True)
        - standard * jnp.mean(scaled * standard, axis=1, keepdims=True)
    )


def column_sum(rows):
    return jnp.sum(rows, axis=0, keepdims=True)


def head_lanes(block, head):
    lane = lax.broadcasted_iota(jnp.int32, block.shape, 1) // HEAD
    return jnp.where(lane == head, block.astype(f32), 0.0).astype(bf16)


V_ASK, V_CONTENT, V_MIXER, V_NARROW, V_G1, V_O1, V_G2, V_O2 = range(8)


def row_of(table_ref, index):
    return table_ref[index : index + 1, :]


def whole(shape):
    return pl.BlockSpec(shape, lambda *_: (0,) * len(shape))


def once(shape):
    return pl.BlockSpec(shape, lambda *_: (0,) * len(shape), pipeline_mode=pl.Buffered(1))


def short_qkv_kernel(x_ref, w_ref, vec_ref, n1_ref, q_ref, k_ref, v_ref, kt_ref, vt_ref):
    standard, _ = standardize(x_ref[...].astype(f32))
    normed = (standard * row_of(vec_ref, V_G1) + row_of(vec_ref, V_O1)).astype(bf16)
    n1_ref[...] = normed
    projected = dot(normed, w_ref[...])
    q = (projected[:, :WIDTH] + row_of(vec_ref, V_ASK)).astype(bf16)
    q_ref[...] = (q.astype(f32) * (1.0 / math.sqrt(HEAD))).astype(bf16)
    k = projected[:, WIDTH : 2 * WIDTH]
    v = projected[:, 2 * WIDTH :] + row_of(vec_ref, V_CONTENT)
    k_ref[...] = k.astype(bf16)
    v_ref[...] = v.astype(bf16)
    kt_ref[...] = k.T.astype(bf16)
    vt_ref[...] = v.T.astype(bf16)


def short_qkv(rows, weights, vectors):
    count = rows.shape[0] - LONG
    block = 256
    row_spec = pl.BlockSpec((block, WIDTH), lambda i: (i, 0))
    col_spec = pl.BlockSpec((WIDTH, block), lambda i: (0, i))
    flat = jax.ShapeDtypeStruct((count, WIDTH), bf16)
    tall = jax.ShapeDtypeStruct((WIDTH, count), bf16)
    return pl.pallas_call(
        short_qkv_kernel,
        grid=(count // block,),
        in_specs=[
            pl.BlockSpec((block, WIDTH), lambda i: (i + LONG // block, 0)),
            whole((WIDTH, 3 * WIDTH)),
            whole(vectors.shape),
        ],
        out_specs=[row_spec, row_spec, row_spec, row_spec, col_spec, col_spec],
        out_shape=[flat, flat, flat, flat, tall, tall],
        compiler_params=pltpu.CompilerParams(**PARAMS),
        cost_estimate=pl.CostEstimate(
            flops=2 * count * WIDTH * 3 * WIDTH, bytes_accessed=6 << 20, transcendentals=0
        ),
        name="short_qkv",
    )(rows, weights, vectors)


def short_forward_kernel(
    q_ref, k_ref, vt_ref, idc_ref, idr_ref, e_ref, o_ref, linv_ref, att_ref, s_ref, bias_ref, top_ref
):
    step = pl.program_id(0)
    count = k_ref.shape[0]
    tile = 256

    @pl.when(step == 0)
    def _():
        same = idc_ref[...] == idr_ref[...]
        bias_ref[...] = jnp.where(same, 0.0, -1e30)

    def first(slot):
        masked = head_lanes(q_ref[...], lax.rem(step, 4))
        top = None
        for low in range(0, count, tile):
            s = dot(k_ref[low : low + tile, :], masked, 1, 1) + bias_ref[low : low + tile, :]
            s_ref[slot, low : low + tile, :] = s
            part = jnp.max(s, axis=0, keepdims=True)
            top = part if top is None else jnp.maximum(top, part)
        top_ref[slot] = jnp.broadcast_to(top, (8, count))

    def second(slot):
        head = step - 1
        top = top_ref[slot, 0:1, :]
        mixed = jnp.zeros((HEAD, count), f32)
        total = jnp.zeros((1, count), f32)
        for low in range(0, count, tile):
            e = jnp.exp(s_ref[slot, low : low + tile, :] - top)
            total += column_sum(e)
            low_e = e.astype(bf16)
            e_ref[low : low + tile, :] = low_e
            mixed += dot(vt_ref[pl.ds(pl.multiple_of(head * HEAD, HEAD), HEAD), low : low + tile], low_e)
        linv = 1.0 / total
        linv_ref[...] = jnp.broadcast_to(linv, (8, count))
        o_ref[pl.ds(pl.multiple_of(head * HEAD, HEAD), HEAD), :] = mixed * linv

    last = pl.num_programs(0) - 1

    @pl.when(step == 0)
    def _():
        first(0)

    for parity in (0, 1):
        @pl.when((step > 0) & (step < last) & (lax.rem(step, 2) == parity))
        def _():
            first(parity)
            second(1 - parity)

    @pl.when(step == last)
    def _():
        second((HEADS - 1) % 2)
        for low in range(0, WIDTH, 128):
            att_ref[:, low : low + 128] = o_ref[low : low + 128, :].T.astype(bf16)


def short_forward(q, k, vt, ids):
    count = q.shape[0]
    now = lambda s: (0, jnp.minimum(s, HEADS - 1) // 4)
    before = lambda s: (0, jnp.maximum(s - 1, 0))
    return pl.pallas_call(
        short_forward_kernel,
        grid=(HEADS + 1,),
        in_specs=[
            pl.BlockSpec((count, GROUP), now),
            pl.BlockSpec((count, GROUP), now),
            whole((WIDTH, count)),
            whole((count, 1)),
            whole((1, count)),
        ],
        out_specs=[
            pl.BlockSpec((count, count), before),
            whole((WIDTH, count)),
            pl.BlockSpec((8, count), lambda s: (jnp.maximum(s - 1, 0), 0)),
            whole((count, WIDTH)),
        ],
        out_shape=[
            jax.ShapeDtypeStruct((count, HEADS * count), bf16),
            jax.ShapeDtypeStruct((WIDTH, count), f32),
            jax.ShapeDtypeStruct((HEADS * 8, count), f32),
            jax.ShapeDtypeStruct((count, WIDTH), bf16),
        ],
        scratch_shapes=[
            pltpu.VMEM((2, count, count), f32),
            pltpu.VMEM((count, count), f32),
            pltpu.VMEM((2, 8, count), f32),
        ],
        compiler_params=pltpu.CompilerParams(**PARAMS),
        cost_estimate=pl.CostEstimate(
            flops=12 * count * count * WIDTH, bytes_accessed=12 << 20, transcendentals=HEADS * count * count
        ),
        name="short_forward",
    )(q, k, vt, ids[:, None], ids[None, :])


def long_prepare_kernel(place_ref, x_ref, w_ref, vec_ref, q_ref, k_ref, v_ref, kt_ref, vt_ref):
    step = pl.program_id(0)
    core = place_ref[1]
    lanes = lambda base: pl.ds(pl.multiple_of(base + core * GROUP, GROUP), GROUP)
    standard, _ = standardize(x_ref[...].astype(f32))
    normed = (standard * row_of(vec_ref, V_G1) + row_of(vec_ref, V_O1)).astype(bf16)
    k = dot(normed, w_ref[:, lanes(WIDTH)])
    v = dot(normed, w_ref[:, lanes(2 * WIDTH)]) + vec_ref[V_CONTENT : V_CONTENT + 1, lanes(0)]
    k_ref[...] = k.astype(bf16)
    v_ref[...] = v.astype(bf16)
    kt_ref[...] = k.T.astype(bf16)
    vt_ref[...] = v.T.astype(bf16)

    @pl.when(step == place_ref[0])
    def _():
        q = (dot(normed, w_ref[:, lanes(0)]) + vec_ref[V_ASK : V_ASK + 1, lanes(0)]).astype(bf16)
        q_ref[...] = (q.astype(f32) * (1.0 / math.sqrt(HEAD))).astype(bf16)


def long_prepare(place, rows, weights, vectors):
    total = rows.shape[0]
    row_spec = pl.BlockSpec((TILE, GROUP), lambda i, _: (i, 0))
    col_spec = pl.BlockSpec((GROUP, TILE), lambda i, _: (0, i))
    flat = jax.ShapeDtypeStruct((total, GROUP), bf16)
    tall = jax.ShapeDtypeStruct((GROUP, total), bf16)
    return pl.pallas_call(
        long_prepare_kernel,
        grid_spec=pltpu.PrefetchScalarGridSpec(
            num_scalar_prefetch=1,
            grid=(total // TILE,),
            in_specs=[
                pl.BlockSpec((TILE, WIDTH), lambda i, _: (i, 0)),
                whole((WIDTH, 3 * WIDTH)),
                whole(vectors.shape),
            ],
            out_specs=[whole((TILE, GROUP)), row_spec, row_spec, col_spec, col_spec],
        ),
        out_shape=[jax.ShapeDtypeStruct((TILE, GROUP), bf16), flat, flat, tall, tall],
        compiler_params=pltpu.CompilerParams(**PARAMS),
        cost_estimate=pl.CostEstimate(
            flops=4 * total * WIDTH * GROUP, bytes_accessed=14 << 20, transcendentals=0
        ),
        name="long_prepare",
    )(place, rows, weights, vectors)


CHUNK = 256
PARTS = TILE // CHUNK
LOCAL_HEADS = GROUP // HEAD
STEPS = LOCAL_HEADS * PARTS


def long_forward_kernel(q_ref, k_ref, vt_ref, e_ref, o_ref, linv_ref, att_ref, s_ref, top_ref):
    step = pl.program_id(0)
    total = k_ref.shape[0]
    tile = 512
    last = pl.num_programs(0) - 1

    def masked_queries():
        rows = pl.ds(pl.multiple_of(lax.rem(step, PARTS) * CHUNK, CHUNK), CHUNK)
        return head_lanes(q_ref[rows, :], step // PARTS)

    def first_tile(slot, low, masked, top):
        s = dot(k_ref[pl.ds(low, tile), :], masked, 1, 1)
        s_ref[slot, pl.ds(low, tile), :] = s
        return jnp.maximum(top, jnp.max(s.reshape(tile // 8, 8, CHUNK), axis=0))

    def second_tile(slot, low, top, head, carry):
        summed, mixed = carry
        e = jnp.exp(s_ref[slot, pl.ds(low, tile), :] - top)
        summed = summed + jnp.sum(e.reshape(tile // 8, 8, CHUNK), axis=0)
        low_e = e.astype(bf16)
        e_ref[pl.ds(low, tile), :] = low_e
        values = vt_ref[pl.ds(pl.multiple_of(head * HEAD, HEAD), HEAD), pl.ds(low, tile)]
        return summed, mixed + dot(values, low_e)

    start_top = jnp.full((8, CHUNK), -1e30, f32)
    start_sum = (jnp.zeros((8, CHUNK), f32), jnp.zeros((HEAD, CHUNK), f32))

    def finish(head, part, carry):
        summed, mixed = carry
        linv = 1.0 / column_sum(summed)
        linv_ref[...] = jnp.broadcast_to(linv, (8, CHUNK))
        o_ref[part, pl.ds(pl.multiple_of(head * HEAD, HEAD), HEAD), :] = mixed * linv

    def place(turn):
        return pl.multiple_of(turn * tile, tile)

    @pl.when(step == 0)
    def _():
        masked = masked_queries()
        top_ref[0] = lax.fori_loop(
            0, total // tile, lambda t, top: first_tile(0, place(t), masked, top), start_top
        )

    for parity in (0, 1):
        @pl.when((step > 0) & (step < last) & (lax.rem(step, 2) == parity))
        def _():
            masked = masked_queries()
            before = step - 1
            head = before // PARTS
            top_row = jnp.max(top_ref[1 - parity], axis=0, keepdims=True)

            def body(turn, carry):
                top, kept = carry
                low = place(turn)
                top = first_tile(parity, low, masked, top)
                kept = second_tile(1 - parity, low, top_row, head, kept)
                return top, kept

            top, kept = lax.fori_loop(0, total // tile, body, (start_top, start_sum))
            top_ref[parity] = top
            finish(head, lax.rem(before, PARTS), kept)

    @pl.when(step == last)
    def _():
        slot = (STEPS - 1) % 2
        top_row = jnp.max(top_ref[slot], axis=0, keepdims=True)
        head = LOCAL_HEADS - 1
        kept = lax.fori_loop(
            0,
            total // tile,
            lambda t, carry: second_tile(slot, place(t), top_row, head, carry),
            start_sum,
        )
        finish(head, PARTS - 1, kept)
        for part in range(PARTS):
            att_ref[part * CHUNK : (part + 1) * CHUNK, :] = o_ref[part].T.astype(bf16)


def long_forward(q, k, vt):
    total = k.shape[0]
    before = lambda s: jnp.maximum(s - 1, 0)
    return pl.pallas_call(
        long_forward_kernel,
        grid=(STEPS + 1,),
        in_specs=[once((TILE, GROUP)), once((total, GROUP)), once((GROUP, total))],
        out_specs=[
            pl.BlockSpec((total, CHUNK), lambda s: (0, before(s))),
            whole((PARTS, GROUP, CHUNK)),
            pl.BlockSpec((8, CHUNK), lambda s: (before(s), 0)),
            whole((TILE, GROUP)),
        ],
        out_shape=[
            jax.ShapeDtypeStruct((total, STEPS * CHUNK), bf16),
            jax.ShapeDtypeStruct((PARTS, GROUP, CHUNK), f32),
            jax.ShapeDtypeStruct((STEPS * 8, CHUNK), f32),
            jax.ShapeDtypeStruct((TILE, GROUP), bf16),
        ],
        scratch_shapes=[pltpu.VMEM((2, total, CHUNK), f32), pltpu.VMEM((2, 8, CHUNK), f32)],
        compiler_params=pltpu.CompilerParams(**PARAMS),
        cost_estimate=pl.CostEstimate(
            flops=16 * TILE * total * GROUP, bytes_accessed=24 << 20, transcendentals=4 * TILE * total
        ),
        name="long_forward",
    )(q, k, vt)


def feed_kernel(
    x_ref, ids_ref, g_ref, att_long_ref, att_short_ref, wp_ref, we_ref, wr_ref, vec_ref, hid_ref,
    out_ref, mid_ref, da_ref, gp_ref, ge_ref, gr_ref, row_ref, hsum_ref, accp, acce, accr,
):
    step = pl.program_id(0)

    @pl.when(step == 0)
    def _():
        accp[...] = jnp.zeros_like(accp)
        acce[...] = jnp.zeros_like(acce)
        accr[...] = jnp.zeros_like(accr)
        row_ref[...] = jnp.zeros_like(row_ref)
        hsum_ref[...] = jnp.zeros_like(hsum_ref)

    x = x_ref[...].astype(f32)
    live = (ids_ref[...] >= 0).astype(f32)
    upstream = g_ref[...].astype(f32)
    attended = jnp.where(step == 0, att_long_ref[...], att_short_ref[...])
    branch = dot(attended, wp_ref[...]) + row_of(vec_ref, V_MIXER)
    middle = x + live * branch
    standard, inverse = standardize(middle)
    gain = row_of(vec_ref, V_G2)
    normed = (standard * gain + row_of(vec_ref, V_O2)).astype(bf16)
    hidden = dot(normed, we_ref[...]) + hid_ref[...]
    square = hidden * hidden
    tangent = jnp.tanh(hidden * (gelu_scale + (gelu_scale * 0.044715) * square))
    half = 0.5 * (1.0 + tangent)
    active = (hidden * half).astype(bf16)
    slope = half + (0.5 * hidden) * (1.0 - tangent * tangent) * (
        gelu_scale + (gelu_scale * 3.0 * 0.044715) * square
    )
    branch_two = dot(active, wr_ref[...]) + row_of(vec_ref, V_NARROW)
    out_ref[...] = (middle + live * branch_two).astype(bf16)
    branch_grad = live * upstream
    branch_low = branch_grad.astype(bf16)
    accr[...] += dot(active, branch_low, 0, 0)
    hidden_grad = dot(branch_low, wr_ref[...], 1, 1) * slope
    hidden_low = hidden_grad.astype(bf16)
    hsum_ref[...] += column_sum(hidden_low.astype(f32))
    acce[...] += dot(normed, hidden_low, 0, 0)
    normed_grad = dot(hidden_low, we_ref[...], 1, 1)
    middle_grad = upstream + norm_backward(normed_grad, standard, inverse, gain)
    mid_ref[...] = middle_grad
    attn_low = (live * middle_grad).astype(bf16)
    accp[...] += dot(attended, attn_low, 0, 0)
    da_ref[...] = dot(attn_low, wp_ref[...], 1, 1).astype(bf16)
    row_ref[0:1, :] += column_sum(attn_low.astype(f32))
    row_ref[1:2, :] += column_sum(branch_low.astype(f32))
    row_ref[2:3, :] += column_sum(normed_grad * standard)
    row_ref[3:4, :] += column_sum(normed_grad)

    @pl.when(step == pl.num_programs(0) - 1)
    def _():
        gp_ref[...] = accp[...].astype(bf16)
        ge_ref[...] = acce[...].astype(bf16)
        gr_ref[...] = accr[...].astype(bf16)


def feed(rows, ids, upstream, att_long, att_short, wp, we, wr, vectors, hidden_shift):
    count = rows.shape[0]
    block = LONG
    row_spec = pl.BlockSpec((block, WIDTH), lambda i: (i, 0))
    return pl.pallas_call(
        feed_kernel,
        grid=(count // block,),
        in_specs=[
            row_spec,
            pl.BlockSpec((block, 1), lambda i: (i, 0)),
            row_spec,
            whole((block, WIDTH)),
            pl.BlockSpec((block, WIDTH), lambda i: (jnp.maximum(i - 1, 0), 0)),
            once((WIDTH, WIDTH)),
            once((WIDTH, FF)),
            once((FF, WIDTH)),
            whole(vectors.shape),
            whole((1, FF)),
        ],
        out_specs=[
            row_spec,
            row_spec,
            row_spec,
            once((WIDTH, WIDTH)),
            once((WIDTH, FF)),
            once((FF, WIDTH)),
            whole((8, WIDTH)),
            whole((1, FF)),
        ],
        out_shape=[
            jax.ShapeDtypeStruct((count, WIDTH), bf16),
            jax.ShapeDtypeStruct((count, WIDTH), f32),
            jax.ShapeDtypeStruct((count, WIDTH), bf16),
            jax.ShapeDtypeStruct((WIDTH, WIDTH), bf16),
            jax.ShapeDtypeStruct((WIDTH, FF), bf16),
            jax.ShapeDtypeStruct((FF, WIDTH), bf16),
            jax.ShapeDtypeStruct((8, WIDTH), f32),
            jax.ShapeDtypeStruct((1, FF), f32),
        ],
        scratch_shapes=[
            pltpu.VMEM((WIDTH, WIDTH), f32),
            pltpu.VMEM((WIDTH, FF), f32),
            pltpu.VMEM((FF, WIDTH), f32),
        ],
        compiler_params=pltpu.CompilerParams(**PARAMS),
        cost_estimate=pl.CostEstimate(
            flops=6 * count * WIDTH * (WIDTH + 2 * FF), bytes_accessed=18 << 20, transcendentals=count * FF
        ),
        name="feed",
    )(rows, ids[:, None], upstream, att_long, att_short, wp, we, wr, vectors, hidden_shift)


def long_backward_kernel(
    place_ref, e_ref, k_ref, v_ref, kt_ref, x_ref, q_ref, da_ref, o_ref, linv_ref, w_ref, vec_ref,
    dx_ref, gq_ref, gkv_ref, row_ref, side_ref,
    qblk, dblk, delta, ds_ref, dq_acc, wq, wkv,
):
    step = pl.program_id(0)
    last = pl.num_programs(0) - 1
    core = place_ref[1]

    @pl.when(step == 0)
    def _():
        lanes = lambda base: pl.ds(pl.multiple_of(base + core * GROUP, GROUP), GROUP)
        wq[...] = w_ref[:, lanes(0)]
        wkv[:, :GROUP] = w_ref[:, lanes(WIDTH)]
        wkv[:, GROUP:] = w_ref[:, lanes(2 * WIDTH)]
        dq_acc[...] = jnp.zeros_like(dq_acc)
        gkv_ref[...] = jnp.zeros_like(gkv_ref)
        row_ref[...] = jnp.zeros_like(row_ref)
        side_ref[...] = jnp.zeros_like(side_ref)
        for part in range(PARTS):
            rows = slice(part * CHUNK, (part + 1) * CHUNK)
            turned = da_ref[rows, :].astype(f32).T
            product = turned * o_ref[part]
            pieces = []
            for head in range(LOCAL_HEADS):
                index = head * PARTS + part
                span = slice(head * HEAD, (head + 1) * HEAD)
                linv = linv_ref[8 * index : 8 * index + 1, :]
                delta[8 * index : 8 * index + 8, :] = jnp.broadcast_to(
                    column_sum(product[span, :]) * linv, (8, CHUNK)
                )
                pieces.append(turned[span, :] * linv)
            scaled = jnp.concatenate(pieces, axis=0).T
            for head in range(LOCAL_HEADS):
                index = head * PARTS + part
                span = slice(index * CHUNK, (index + 1) * CHUNK)
                dblk[span, :] = head_lanes(scaled, head)
                qblk[span, :] = head_lanes(q_ref[rows, :], head)

    for head in range(LOCAL_HEADS):
        for part in range(PARTS):
            index = head * PARTS + part
            span = slice(index * CHUNK, (index + 1) * CHUNK)
            slopes = dot(v_ref[...], dblk[span, :], 1, 1)
            ds = (
                e_ref[:, span].astype(f32) * (slopes - delta[8 * index : 8 * index + 1, :])
            ).astype(bf16)
            ds_ref[:, span] = ds
            own = slice(head * HEAD, (head + 1) * HEAD)
            dq_acc[part, own, :] += dot(kt_ref[own, :], ds)

    value_grad = dot(e_ref[...], dblk[...]).astype(bf16)
    key_grad = dot(ds_ref[...], qblk[...]).astype(bf16)
    both = jnp.concatenate([key_grad, value_grad], axis=1)
    standard, _ = standardize(x_ref[...].astype(f32))
    normed = (standard * row_of(vec_ref, V_G1) + row_of(vec_ref, V_O1)).astype(bf16)
    through = dot(both, wkv[...], 1, 1)
    gkv_ref[...] += dot(normed, both, 0, 0)
    side_ref[1:2, :] += column_sum(value_grad.astype(f32))

    @pl.when(step < last)
    def _():
        dx_ref[...] = through.astype(bf16)
        row_ref[0:1, :] += column_sum(through * standard)
        row_ref[1:2, :] += column_sum(through)

    @pl.when(step == last)
    def _():
        query_grad = jnp.concatenate(
            [dq_acc[part].T for part in range(PARTS)], axis=0
        ) * (1.0 / math.sqrt(HEAD))
        low = query_grad.astype(bf16)
        entire = through + dot(low, wq[...], 1, 1)
        dx_ref[...] = entire.astype(bf16)
        row_ref[0:1, :] += column_sum(entire * standard)
        row_ref[1:2, :] += column_sum(entire)
        gq_ref[...] = dot(normed, low, 0, 0)
        side_ref[0:1, :] = column_sum(low.astype(f32))


def long_backward(place, e, k, v, kt, rows, q, da, o, linv, weights, vectors):
    total = k.shape[0]
    tiles = total // TILE
    turn = lambda i, place: lax.rem(place[0] + 1 + i, tiles)
    return pl.pallas_call(
        long_backward_kernel,
        grid_spec=pltpu.PrefetchScalarGridSpec(
            num_scalar_prefetch=1,
            grid=(tiles,),
            in_specs=[
                pl.BlockSpec((TILE, STEPS * CHUNK), lambda i, p: (turn(i, p), 0)),
                pl.BlockSpec((TILE, GROUP), lambda i, p: (turn(i, p), 0)),
                pl.BlockSpec((TILE, GROUP), lambda i, p: (turn(i, p), 0)),
                pl.BlockSpec((GROUP, TILE), lambda i, p: (0, turn(i, p))),
                pl.BlockSpec((TILE, WIDTH), lambda i, p: (turn(i, p), 0)),
                whole((TILE, GROUP)),
                whole((TILE, GROUP)),
                whole((PARTS, GROUP, CHUNK)),
                whole((STEPS * 8, CHUNK)),
                whole((WIDTH, 3 * WIDTH)),
                whole(vectors.shape),
            ],
            out_specs=[
                pl.BlockSpec((TILE, WIDTH), lambda i, p: (turn(i, p), 0)),
                whole((WIDTH, GROUP)),
                whole((WIDTH, 2 * GROUP)),
                whole((8, WIDTH)),
                whole((8, GROUP)),
            ],
            scratch_shapes=[
                pltpu.VMEM((STEPS * CHUNK, GROUP), bf16),
                pltpu.VMEM((STEPS * CHUNK, GROUP), bf16),
                pltpu.VMEM((STEPS * 8, CHUNK), f32),
                pltpu.VMEM((TILE, STEPS * CHUNK), bf16),
                pltpu.VMEM((PARTS, GROUP, CHUNK), f32),
                pltpu.VMEM((WIDTH, GROUP), bf16),
                pltpu.VMEM((WIDTH, 2 * GROUP), bf16),
            ],
        ),
        out_shape=[
            jax.ShapeDtypeStruct((total, WIDTH), bf16),
            jax.ShapeDtypeStruct((WIDTH, GROUP), f32),
            jax.ShapeDtypeStruct((WIDTH, 2 * GROUP), f32),
            jax.ShapeDtypeStruct((8, WIDTH), f32),
            jax.ShapeDtypeStruct((8, GROUP), f32),
        ],
        compiler_params=pltpu.CompilerParams(**PARAMS),
        cost_estimate=pl.CostEstimate(
            flops=40 * TILE * total * GROUP, bytes_accessed=32 << 20, transcendentals=0
        ),
        name="long_backward",
    )(place, e, k, v, kt, rows, q, da, o, linv, weights, vectors)


def short_backward_kernel(
    place_ref, e_ref, k_ref, v_ref, q_ref, kt_ref, da_ref, o_ref, linv_ref, n1_ref, x_ref, mid_ref, w_ref,
    vec_ref, gq_ref, gkv_ref,
    dx_ref, g_ref, row_ref, qv_ref,
    scaled, delta, dblk, qblk, ds_ref, dqt, dqkv,
):
    step = pl.program_id(0)
    count = k_ref.shape[0]

    @pl.when(step == 0)
    def _():
        for low in range(0, WIDTH, GROUP):
            turned = da_ref[:, low : low + GROUP].astype(f32).T
            product = turned * o_ref[low : low + GROUP, :]
            pieces = []
            for head in range(4):
                span = slice(head * HEAD, (head + 1) * HEAD)
                index = low // HEAD + head
                linv = linv_ref[8 * index : 8 * index + 1, :]
                delta[8 * index : 8 * index + 8, :] = jnp.broadcast_to(
                    column_sum(product[span, :]) * linv, (8, count)
                )
                pieces.append(turned[span, :] * linv)
            scaled[:, low : low + GROUP] = jnp.concatenate(pieces, axis=0).T.astype(bf16)

    def group(side):
        low = side * GROUP
        for head in range(4):
            index = side * 4 + head
            span = slice(head * count, (head + 1) * count)
            own = slice(head * HEAD, (head + 1) * HEAD)
            dblk[span, :] = head_lanes(scaled[:, low : low + GROUP], head)
            qblk[span, :] = head_lanes(q_ref[...], head)
            slopes = dot(v_ref[...], dblk[span, :], 1, 1)
            ds = (
                e_ref[:, span].astype(f32) * (slopes - delta[8 * index : 8 * index + 1, :])
            ).astype(bf16)
            ds_ref[:, span] = ds
            dqt[own, :] = dot(kt_ref[low + head * HEAD : low + (head + 1) * HEAD, :], ds)
        value_grad = dot(e_ref[...], dblk[...])
        key_grad = dot(ds_ref[...], qblk[...])
        query_grad = dqt[...].T * (1.0 / math.sqrt(HEAD))
        dqkv[:, low : low + GROUP] = query_grad.astype(bf16)
        dqkv[:, WIDTH + low : WIDTH + low + GROUP] = key_grad.astype(bf16)
        dqkv[:, 2 * WIDTH + low : 2 * WIDTH + low + GROUP] = value_grad.astype(bf16)

    for side in (0, 1):
        pl.when(step == side)(functools.partial(group, side))

    @pl.when(step == 1)
    def _():
        rows_grad = dot(dqkv[...], w_ref[...], 1, 1)
        standard, inverse = standardize(x_ref[...].astype(f32))
        through = norm_backward(rows_grad, standard, inverse, row_of(vec_ref, V_G1))
        dx_ref[...] = (mid_ref[...] + through).astype(bf16)
        row_ref[...] = jnp.zeros_like(row_ref)
        row_ref[0:1, :] = column_sum(rows_grad * standard)
        row_ref[1:2, :] = column_sum(rows_grad)
        qv_ref[...] = jnp.broadcast_to(column_sum(dqkv[...].astype(f32)), qv_ref.shape)
        total = dot(n1_ref[...], dqkv[...], 0, 0)
        g_ref[...] = total.astype(bf16)
        core = place_ref[1]
        for other in (0, 1):
            @pl.when(core == other)
            def _():
                for third in range(3):
                    low = third * WIDTH + other * GROUP
                    extra = gq_ref[...] if third == 0 else gkv_ref[:, (third - 1) * GROUP : third * GROUP]
                    g_ref[:, low : low + GROUP] = (total[:, low : low + GROUP] + extra).astype(bf16)


def short_backward(place, e, k, v, q, kt, da, o, linv, n1, rows, mid, weights, vectors, gq, gkv):
    count = k.shape[0]
    half = pl.BlockSpec((count, GROUP), lambda i, _: (0, i))
    return pl.pallas_call(
        short_backward_kernel,
        grid_spec=pltpu.PrefetchScalarGridSpec(
            num_scalar_prefetch=1,
            grid=(2,),
            in_specs=[
                pl.BlockSpec((count, 4 * count), lambda i, _: (0, i)),
                half,
                half,
                half,
                once((WIDTH, count)),
                once((count, WIDTH)),
                once((WIDTH, count)),
                once((HEADS * 8, count)),
                once((count, WIDTH)),
                once((count, WIDTH)),
                once((count, WIDTH)),
                once((WIDTH, 3 * WIDTH)),
                whole(vectors.shape),
                once((WIDTH, GROUP)),
                once((WIDTH, 2 * GROUP)),
            ],
            out_specs=[
                once((count, WIDTH)),
                once((WIDTH, 3 * WIDTH)),
                whole((8, WIDTH)),
                whole((8, 3 * WIDTH)),
            ],
            scratch_shapes=[
                pltpu.VMEM((count, WIDTH), bf16),
                pltpu.VMEM((HEADS * 8, count), f32),
                pltpu.VMEM((4 * count, GROUP), bf16),
                pltpu.VMEM((4 * count, GROUP), bf16),
                pltpu.VMEM((count, 4 * count), bf16),
                pltpu.VMEM((GROUP, count), f32),
                pltpu.VMEM((count, 3 * WIDTH), bf16),
            ],
        ),
        out_shape=[
            jax.ShapeDtypeStruct((count, WIDTH), bf16),
            jax.ShapeDtypeStruct((WIDTH, 3 * WIDTH), bf16),
            jax.ShapeDtypeStruct((8, WIDTH), f32),
            jax.ShapeDtypeStruct((8, 3 * WIDTH), f32),
        ],
        compiler_params=pltpu.CompilerParams(**PARAMS),
        cost_estimate=pl.CostEstimate(
            flops=24 * count * count * WIDTH, bytes_accessed=18 << 20, transcendentals=0
        ),
        name="short_backward",
    )(place, e, k, v, q, kt, da, o, linv, n1, rows, mid, weights, vectors, gq, gkv)


def per_device(
    incoming_rows,
    picture_label,
    triple_kernel,
    mixer_kernel,
    widening_kernel,
    narrowing_kernel,
    asker_offset,
    content_offset,
    mixer_offset_vector,
    widening_offset,
    narrowing_offset,
    leading_gain,
    leading_offset,
    second_gain,
    second_offset,
    loss_sensitivity,
):
    axes = ("band", "batch")
    band = lax.axis_index("band")
    bands = lax.axis_size("band")
    rows = incoming_rows[0]
    ids = picture_label[0]
    upstream = loss_sensitivity[0]
    shard = triple_kernel.shape[0]
    place = jnp.stack([band // 2, band % 2]).astype(jnp.int32)

    vector_shards = [
        v.astype(bf16)[:, None]
        for v in (
            asker_offset,
            content_offset,
            mixer_offset_vector,
            narrowing_offset,
            leading_gain,
            leading_offset,
            second_gain,
            second_offset,
        )
    ] + [widening_offset.astype(bf16).reshape(shard, 4)]
    vector_shard = jnp.concatenate(vector_shards + [jnp.zeros((shard, 116), bf16)], axis=1)
    first = lax.all_gather(
        jnp.concatenate([triple_kernel.astype(bf16), vector_shard], axis=1), axes, axis=0, tiled=True
    )
    all_rows = lax.all_gather(rows[:LONG], "band", axis=0, tiled=True)
    second = lax.all_gather(
        jnp.concatenate(
            [
                mixer_kernel.astype(bf16),
                widening_kernel.astype(bf16),
                narrowing_kernel.astype(bf16).reshape(4, shard, WIDTH).transpose(1, 0, 2).reshape(shard, FF),
            ],
            axis=1,
        ),
        axes,
        axis=0,
        tiled=True,
    )
    wqkv = first[:, : 3 * WIDTH]
    vectors = first[:, 3 * WIDTH : 3 * WIDTH + 16].T.astype(f32)
    hidden_shift = first[:, 3 * WIDTH + 8 : 3 * WIDTH + 12].reshape(1, FF).astype(f32)
    wp = second[:, :WIDTH]
    we = second[:, WIDTH : WIDTH + FF]
    wr = (
        second[:, WIDTH + FF :]
        .reshape(WIDTH // shard, shard, 4, WIDTH)
        .transpose(0, 2, 1, 3)
        .reshape(FF, WIDTH)
    )

    n1, q_s, k_s, v_s, kt_s, vt_s = short_qkv(rows, wqkv, vectors)
    e_s, o_s, linv_s, att_s = short_forward(q_s, k_s, vt_s, ids[LONG:])
    q_l, k_l, v_l, kt_l, vt_l = long_prepare(place, all_rows, wqkv, vectors)
    e_l, o_l, linv_l, att_l = long_forward(q_l, k_l, vt_l)

    pairs = [(i, i ^ 1) for i in range(bands)]
    even = place[1] == 0
    mine = jnp.where(even, att_l[:LONG], att_l[LONG:])
    other = lax.ppermute(jnp.where(even, att_l[LONG:], att_l[:LONG]), "band", pairs)
    att_long = jnp.concatenate([jnp.where(even, mine, other), jnp.where(even, other, mine)], axis=1)

    layer_out, mid, da, gp, ge, gr, feed_rows, hidden_sum = feed(
        rows, ids, upstream, att_long, att_s, wp, we, wr, vectors, hidden_shift
    )
    da_mine = jnp.where(even, da[:LONG, :GROUP], da[:LONG, GROUP:])
    da_other = lax.ppermute(jnp.where(even, da[:LONG, GROUP:], da[:LONG, :GROUP]), "band", pairs)
    da_l = jnp.concatenate([jnp.where(even, da_mine, da_other), jnp.where(even, da_other, da_mine)], axis=0)

    shards = WIDTH // shard
    second_grad = lax.psum_scatter(
        jnp.concatenate(
            [gp, ge, gr.reshape(shards, 4, shard, WIDTH).transpose(0, 2, 1, 3).reshape(WIDTH, FF)], axis=1
        ),
        axes,
        scatter_dimension=0,
        tiled=True,
    )

    dx, gq, gkv, long_rows, long_side = long_backward(
        place, e_l, k_l, v_l, kt_l, all_rows, q_l, da_l, o_l, linv_l, wqkv, vectors
    )
    dx_long = lax.psum_scatter(dx, "band", scatter_dimension=0, tiled=True)
    dx_s, g_qkv, short_rows, short_side = short_backward(
        place, e_s, k_s, v_s, q_s, kt_s, da[LONG:], o_s, linv_s, n1, rows[LONG:], mid[LONG:], wqkv, vectors, gq, gkv
    )

    spread = lambda row: jnp.where(
        even, jnp.concatenate([row, jnp.zeros_like(row)]), jnp.concatenate([jnp.zeros_like(row), row])
    )
    vector_rows = [
        short_side[0, :WIDTH] + spread(long_side[0]),
        short_side[0, 2 * WIDTH :] + spread(long_side[1]),
        feed_rows[0],
        feed_rows[1],
        short_rows[0] + long_rows[0],
        short_rows[1] + long_rows[1],
        feed_rows[2],
        feed_rows[3],
    ]
    vector_grad = jnp.concatenate(
        [jnp.stack(vector_rows, axis=1), hidden_sum.reshape(WIDTH, 4), jnp.zeros((WIDTH, 116), f32)], axis=1
    ).astype(bf16)
    first_grad = lax.psum_scatter(
        jnp.concatenate([g_qkv, vector_grad], axis=1), axes, scatter_dimension=0, tiled=True
    )

    standard, inverse = standardize(rows[:LONG].astype(f32))
    dx_l = (
        mid[:LONG] + norm_backward(dx_long.astype(f32), standard, inverse, vectors[V_G1][None, :])
    ).astype(bf16)
    input_grad = jnp.concatenate([dx_l, dx_s], axis=0)

    first_grad = first_grad.astype(f32)
    second_grad = second_grad.astype(f32)
    small = first_grad[:, 3 * WIDTH :]
    return (
        layer_out[None],
        input_grad[None],
        first_grad[:, : 3 * WIDTH],
        second_grad[:, :WIDTH],
        second_grad[:, WIDTH : WIDTH + FF],
        second_grad[:, WIDTH + FF :].reshape(shard, 4, WIDTH).transpose(1, 0, 2).reshape(4 * shard, WIDTH),
        small[:, 0],
        small[:, 1],
        small[:, 2],
        small[:, 8:12].reshape(4 * shard),
        small[:, 3],
        small[:, 4],
        small[:, 5],
        small[:, 6],
        small[:, 7],
    )


def solution(mesh):
    shards = P(("band", "batch"))
    tokens = P("batch", "band", None)
    kernels = P(("band", "batch"), None)
    in_specs = (
        (tokens, P("batch", "band")) + (kernels,) * 4 + (shards,) * 9 + (tokens,)
    )
    out_specs = (tokens, tokens) + (kernels,) * 4 + (shards,) * 9
    return jax.shard_map(
        per_device, mesh=mesh, in_specs=in_specs, out_specs=out_specs, check_vma=False
    )
```

time: 1070 us -> 648 us (0.61)
  matrix products: 259 us -> 0 us
  blocking collectives: 157 us -> 0 us
  Pallas kernels: 0 us -> 144 us
  waiting for transfers between devices: 491 us -> 405 us
  local copies, waits for them, and re-layouts: 81.4 us -> 48.2 us
  other arithmetic: 49.8 us -> 26.5 us
    dot_general x58 -> x0, matrix products: 259 us -> none  [the longest x15 61.9 us: score_block(): jnp.einsum('qhd,khd->hqk', queries, key_block, preferred_element_type=jnp...]
    pallas_call x0 -> x7, Pallas kernels: none -> 144 us  [the longest x1 39.9 us: long_backward(): pl.pallas_call(long_backward_kernel, grid_spec=pltpu.PrefetchScalarGridSp...]
    reduce_scatter x5 -> x3, waiting for transfers between devices: 437 us -> 303 us  [the longest x1 127 us: per_device(): lax.psum_scatter(jnp.concatenate([g_qkv, vector_grad], axis=1), axes, sca...]
    unnamed x2 -> x0, blocking collectives: 81.3 us -> none
    all_gather x1 -> x0, blocking collectives: 76.1 us -> none  [per_device(): lax.all_gather(mixer_kernel.astype(jnp.bfloat16), ('band', 'batch'), axis...]
    all_gather x5 -> x3, waiting for transfers between devices: 54 us -> 101 us  [the longest x1 48.9 us: per_device(): lax.all_gather(jnp.concatenate([triple_kernel.astype(bf16), vector_shard]...]
    unnamed x213 -> x19, local copies, waits for them, and re-layouts: 26.2 us -> 2.46 us
    reduce_sum x14 -> x3, other arithmetic: 21 us -> 1.53 us  [the longest x1 1.2 us: norm_backward(): jnp.mean(scaled, axis=1, keepdims=True)]
  transfers between devices with their start and end apart: 10 -> 8, of which waited for: 6 -> 6; matrix products, arithmetic and copies ran while one was open for 23% -> 6% of each run, Pallas kernels for 0% -> 9%
where the time goes in v1:
time: 648 us; the launch traced here: 639 us
  waiting for transfers between devices  405 us (62%)
  Pallas kernels  144 us (22%)
  local copies, waits for them, and re-layouts  48.2 us (7%)
  other arithmetic  26.5 us (4%)
  between operations  14.9 us (2%)
    reduce_scatter x1, waiting for transfers between devices, per_device(): lax.psum_scatter(jnp.concatenate([g_qkv, vector_grad], axis=1), axes, sca...  127 us
    reduce_scatter x1, waiting for transfers between devices, per_device(): lax.psum_scatter(jnp.concatenate([gp, ge, gr.reshape(shards, 4, shard, WI...  105 us
    reduce_scatter x1, waiting for transfers between devices, per_device(): dx_long = lax.psum_scatter(dx, 'band', scatter_dimension=0, tiled=True)  71.5 us
    all_gather x1, waiting for transfers between devices, per_device(): lax.all_gather(jnp.concatenate([triple_kernel.astype(bf16), vector_shard]...  48.9 us
    pallas_call x1, Pallas kernels, long_backward(): pl.pallas_call(long_backward_kernel, grid_spec=pltpu.PrefetchScalarGridSp...  39.9 us
    all_gather x1, waiting for transfers between devices, per_device(): all_rows = lax.all_gather(rows[:LONG], 'band', axis=0, tiled=True)  29.4 us
    pallas_call x1, Pallas kernels, feed(): pl.pallas_call(feed_kernel, grid=(count // block,), in_specs=[row_spec, p...  26.7 us
    pallas_call x1, Pallas kernels, long_forward(): pl.pallas_call(long_forward_kernel, grid=(STEPS + 1,), in_specs=[once((TI...  25.9 us
  transfers between devices with their start and end apart: 8, of which 6 were waited for; matrix products, arithmetic and copies ran while one was open for 6% of the time, Pallas kernels for 9%

profile of v1, /device:TPU:0, one launch (start us, length us, event | category | flops | bytes accessed | tf_op | source)
XLA Modules:
  0.0 639.4 jit_solution(8165686137682008720)
XLA Ops:
  7.2 1.0 convert_element_type.65
  9.0 0.7 convert_bitcast_fusion.10
  9.7 0.7 convert_bitcast_fusion.9
  10.5 0.7 convert_bitcast_fusion.8
  11.3 0.7 convert_bitcast_fusion.7
  12.8 0.7 convert_bitcast_fusion.5
  15.0 0.7 concatenate.36
  15.8 1.7 slice.152
  17.6 0.9 convert_element_type.79
  18.6 0.9 convert_element_type.78
  19.5 0.8 convert_element_type.77
  20.3 0.7 pad_maximum_fusion.3
  21.6 0.9 copy.71.idc_ref
  22.6 1.0 copy.74.ids_ref
  24.2 1.0 slice_bitcast_fusion.x_ref
  25.2 48.9 %all-gather.5.cloned.1.call-done = bf16[512,1664]{1,0:T(8,128)(2,1)} async-done(((bf16[16,1664]{1,0:T(8,128)(2,1)}), bf16[512,1664]{1,0:T(8,128)(2,1)}) %all-gather.5.cloned.1.call-update) | async-done | bytes 1703952 | tf_op jit(solution)/shard_map/all_gather | solution.py:772
  74.1 0.9 slice.197
  75.1 2.7 slice.196.w_ref
  78.4 5.3 short_qkv.1
  83.7 12.7 %short_forward.1 = (bf16[768,6144]{1,0:T(8,128)(2,1)}, f32[512,768]{1,0:T(8,128)}, f32[64,768]{1,0:T(8,128)}, bf16[768,512]{1,0:T(8,128)(2,1)}) custom-call(bf16[768,512]{1,0:T(8,128)(2,1)} %get-tuple-element.55.q_ref, bf16[768,512]{1,0:T(8,128)(2,1)} %get-tuple-element.56.k_ref, bf16[512,768]{1,0:T(8,128)(2,1)} %get-tuple-element.57.vt_ref, ...), custom_call_target="tpu_custom_call" | custom-call | flops 3623878656 | bytes 12582912 | tf_op jit(solution)/shard_map/short_forward/pallas_call | solution.py:168
  96.3 29.4 %all-gather.9.cloned.1.call-done = bf16[1,4096,512]{2,1,0:T(8,128)(2,1)} async-done(((bf16[1,256,512]{2,1,0:T(8,128)(2,1)}), bf16[1,4096,512]{2,1,0:T(8,128)(2,1)}) %all-gather.9.cloned.1.call-update) | async-done | bytes 4194320 | tf_op jit(solution)/shard_map/all_gather | solution.py:775
  125.7 12.1 %long_prepare.1 = (bf16[512,256]{1,0:T(8,128)(2,1)}, bf16[4096,256]{1,0:T(8,128)(2,1)}, bf16[4096,256]{1,0:T(8,128)(2,1)}, bf16[256,4096]{1,0:T(8,128)(2,1)}, bf16[256,4096]{1,0:T(8,128)(2,1)}) custom-call(s32[2]{0:T(128)} %pad_add_fusion.place_ref, bf16[4096,512]{1,0:T(8,128)(2,1)} %bitcast.105, bf16[512,1536]{1,0:T(8,128)(2,1)} %slice.196.w_ref, ...), custom_call_target="tpu_custom_call" | custom-call | flops 2147483648 | bytes 14680064 | tf_op jit(solution)/shard_map/long_prepare/pallas_call | solution.py:228
  137.8 25.9 %long_forward.1 = (bf16[4096,2048]{1,0:T(8,128)(2,1)}, f32[2,256,256]{2,1,0:T(8,128)}, f32[64,256]{1,0:T(8,128)}, bf16[512,256]{1,0:T(8,128)(2,1)}) custom-call(bf16[512,256]{1,0:T(8,128)(2,1)} %get-tuple-element.51.q_ref, bf16[4096,256]{1,0:T(8,128)(2,1)} %get-tuple-element.52.k_ref, bf16[256,4096]{1,0:T(8,128)(2,1)} %get-tuple-element.53.vt_ref), custom_call_target="tpu_custom_call" | custom-call | flops 8589934592 | bytes 25165824 | tf_op jit(solution)/shard_map/long_forward/pallas_call | solution.py:336
  163.7 1.0 broadcast_select_fusion.6
  165.0 1.0 slice_convert_fusion
  166.0 0.8 reshape.153.hid_ref
  166.8 1.0 broadcast_select_fusion.5
  167.8 0.7 pad_maximum_fusion.1.att_long_ref
  168.6 22.3 %all-gather.7.cloned.1.call-done = bf16[512,4608]{1,0:T(8,128)(2,1)} async-done(((bf16[16,4608]{1,0:T(8,128)(2,1)}), bf16[512,4608]{1,0:T(8,128)(2,1)}) %all-gather.7.cloned.1.call-update) | async-done | bytes 4718608 | tf_op jit(solution)/shard_map/all_gather | solution.py:776
  190.8 4.8 fusion.12
  195.6 3.3 reshape.145
  199.0 1.9 copy.73
  200.9 1.9 slice.198.wp_ref
  202.8 26.7 %feed.1 = (bf16[1024,512]{1,0:T(8,128)(2,1)}, f32[1024,512]{1,0:T(8,128)}, bf16[1024,512]{1,0:T(8,128)(2,1)}, bf16[512,512]{1,0:T(8,128)(2,1)}, bf16[512,2048]{1...) custom-call(bf16[1024,512]{1,0:T(8,128)(2,1)} %bitcast.90, ...), custom_call_target="tpu_custom_call" | custom-call | flops 14495514624 | bytes 18874368 | tf_op jit(solution)/shard_map/feed/pallas_call | solution.py:423
  229.5 1.0 broadcast_select_fusion.2
  230.8 0.7 convert.40
  231.6 2.1 slice.167.da_ref
  233.7 2.7 slice.170.mid_ref
  237.5 1.0 broadcast_select_fusion.1
  238.5 0.7 pad_maximum_fusion.2.da_ref
  239.2 39.9 %long_backward.1 = (bf16[4096,512]{1,0:T(8,128)(2,1)}, f32[512,256]{1,0:T(8,128)}, f32[512,512]{1,0:T(8,128)}, f32[8,512]{1,0:T(8,128)}, f32[8,256]{1,0:T(8,128)}) custom-call(s32[2]{0:T(128)} %pad_add_fusion.place_ref, bf16[4096,2048]{1,0:T(8,128)(2,1)} %get-tuple-element.61.e_ref, bf16[4096,256]{1,0:T(8,128)(2,1)} %get-tuple-element.52.k_ref, ...), custom_call_target="tpu_custom_call" | custom-call | flops 21474836480 | bytes 33554432 | tf_op jit(solution)/shard_map/long_backward/pallas_call | solution.py:555
  279.2 21.8 %short_backward.1 = (bf16[768,512]{1,0:T(8,128)(2,1)}, bf16[512,1536]{1,0:T(8,128)(2,1)}, f32[8,512]{1,0:T(8,128)}, f32[8,1536]{1,0:T(8,128)}) custom-call(s32[2]{0:T(128)} %pad_add_fusion.place_ref, bf16[768,6144]{1,0:T(8,128)(2,1)} %get-tuple-element.68.e_ref, bf16[768,512]{1,0:T(8,128)(2,1)} %get-tuple-element.56.k_ref, ...), custom_call_target="tpu_custom_call" | custom-call | flops 7247757312 | bytes 18874368 | tf_op jit(solution)/shard_map/short_backward/pallas_call | solution.py:679
  301.0 0.8 convert_bitcast_fusion.2
  302.2 0.7 fusion.14
  302.9 0.8 fusion.15
  304.0 4.5 concatenate.45
  308.6 2.0 copy.83
  311.3 0.9 copy-done.3
  312.3 2.4 pad_maximum_fusion
  315.3 0.7 copy-done.1
  316.3 0.7 slice.202
  317.1 126.6 %reduce-scatter.6.cloned.1.call-done = bf16[16,1664]{1,0:T(8,128)(2,1)} async-done(((bf16[512,1664]{1,0:T(8,128)(2,1)}), bf16[16,1664]{1,0:T(8,128)(2,1)}) %reduce-scatter.6.cloned.1.call-update) | async-done | bytes 53264 | tf_op jit(solution)/shard_map/reduce_scatter | solution.py:853
  443.7 0.8 slice.214
  445.0 0.8 convert_element_type.85
  445.8 1.4 slice.207
  447.3 0.8 slice_reduce_fusion
  448.1 105.2 %reduce-scatter.8.cloned.1.call-done = bf16[16,4608]{1,0:T(8,128)(2,1)} async-done(((bf16[512,4608]{1,0:T(8,128)(2,1)}), bf16[16,4608]{1,0:T(8,128)(2,1)}) %reduce-scatter.8.cloned.1.call-update) | async-done | bytes 147472 | tf_op jit(solution)/shard_map/reduce_scatter | solution.py:820
  553.3 1.5 fusion.13
  555.0 0.7 copy.84
  555.6 1.3 slice.208
  557.0 71.5 %reduce-scatter.4.cloned.1.call-done = bf16[256,512]{1,0:T(8,128)(2,1)} async-done(((bf16[4096,512]{1,0:T(8,128)(2,1)}), bf16[256,512]{1,0:T(8,128)(2,1)}) %reduce-scatter.4.cloned.1.call-update) | async-done | bytes 262160 | tf_op jit(solution)/shard_map/reduce_scatter | solution.py:832
  628.5 1.2 fusion.11
  629.7 1.4 fusion.9
  631.1 1.0 maximum_bitcast_fusion
  (71 shorter events, 10.5 us)
Async XLA Ops:
  7.2 17.0 %copy-start = (bf16[1,1024,512]{2,1,0:T(8,128)(2,1)S(1)}, bf16[1,1024,512]{2,1,0:T(8,128)(2,1)}, u32[]{:S(2)}) copy-start(bf16[1,1024,512]{2,1,0:T(8,128)(2,1)} %param.16) | copy-start | bytes 3145732
  7.2 13.8 %copy-start.6 = (s32[1,1024]{1,0:T(1,128)S(1)}, s32[1,1024]{1,0:T(1,128)}, u32[]{:S(2)}) copy-start(s32[1,1024]{1,0:T(1,128)} %param.17) | copy-start | bytes 12292
  7.2 66.9 %all-gather.5.cloned.1.call-start = ((), (), s32[]{:S(2)}) async-start(), calls=%async_computation.3 | async-start | bytes 1757184 | tf_op jit(solution)/shard_map/all_gather | solution.py:772
  15.8 109.9 %all-gather.9.cloned.1.call-start = ((), (), s32[]{:S(2)}) async-start(), calls=%async_computation.8 | async-start | bytes 4456448 | tf_op jit(solution)/shard_map/all_gather | solution.py:775
  17.5 173.3 %all-gather.7.cloned.1.call-start = ((), (), s32[]{:S(2)}) async-start(), calls=%async_computation.4 | async-start | bytes 4866048 | tf_op jit(solution)/shard_map/all_gather | solution.py:776
  21.0 422.7 %reduce-scatter.6.cloned.1.call-start = ((), (), s32[]{:S(2)}) async-start(), calls=%async_computation.6 | async-start | bytes 1757184 | tf_op jit(solution)/shard_map/reduce_scatter | solution.py:853
  164.7 2.2 collective-permute-start
  230.5 7.0 %collective-permute-start.1 = (bf16[256,256]{1,0:T(8,128)(2,1)S(1)}, bf16[256,256]{1,0:T(8,128)(2,1)S(1)}, u32[]{:S(2)}, u32[]{:S(2)}) collective-permute-start(bf16[256,256]{1,0:T(8,128)(2,1)S(1)} %broadcast_select_fusion.2), channel_id=1, source_target_pairs={{0,2},{2,0},{4,6},{6,4},{8,10},{10,8},{12,14},{14,12},{16,18},{18,... | collective-permute-start | bytes 393224 | tf_op jit(solution)/shard_map/ppermute | solution.py:816
  233.7 3.5 copy-start.7
  304.0 4.6 copy-start.2
  308.6 244.7 %reduce-scatter.8.cloned.1.call-start = ((), (), s32[]{:S(2)}) async-start(), calls=%async_computation.7 | async-start | bytes 4866048 | tf_op jit(solution)/shard_map/reduce_scatter | solution.py:820
  310.6 1.6 copy-start.3
  310.6 1.7 copy-start.5
  314.7 313.8 %reduce-scatter.4.cloned.1.call-start = ((), (), s32[]{:S(2)}) async-start(), calls=%async_computation.5 | async-start | bytes 4456448 | tf_op jit(solution)/shard_map/reduce_scatter | solution.py:832
  314.8 1.2 copy-start.1
  316.0 315.1 %copy-start.4 = (bf16[768,512]{1,0:T(8,128)(2,1)S(1)}, bf16[768,512]{1,0:T(8,128)(2,1)}, u32[]{:S(2)}) copy-start(bf16[768,512]{1,0:T(8,128)(2,1)} %get-tuple-element.76) | copy-start | bytes 2359300
Sparse Core Ops, SparseCore 0:
  15.9 58.1 all-gather.4
  76.2 49.4 all-gather.8
  128.6 62.1 all-gather.6
  308.7 134.9 reduce-scatter.5
  449.9 103.3 reduce-scatter.7
  557.0 71.4 reduce-scatter.3
